TPU v7x, 32 devices: a whole 2x2x4 slice. The times are simulated.
32 devices in a mesh: blk: 16 (over z, y, x), rep: 2 (over core).
Axes of the slice: x: 2, y: 2, z: 4, core: 2. Of those that a mesh axis runs over, the one named last changes fastest.
Arguments:
- grad_out: bfloat16 [4096, 256], P(('blk', 'rep')), may hold values from -6 to 6
- preact: bfloat16 [4096, 256], P(('blk', 'rep')), may hold values from -6 to 6
- aggregated: bfloat16 [4096, 256], P(('blk', 'rep')), may hold values from -6 to 6
- weight: bfloat16 [256, 256], replicated, may hold values from -0.375 to 0.375
- degree: int32 [4096], P(('blk', 'rep')), may hold values from 4 to 64
- neighbors: int32 [16, 2, 16, 2, 8, 128], P('blk', 'rep'), may hold values from 0 to 127
- tile_col: int32 [16, 2, 16, 2], P('blk', 'rep'), may hold values from 0 to 1, as said below
- tile_count: int32 [16, 2, 16], P('blk', 'rep'), may hold values from 0 to 2, as said below
Outputs:
- grad_features: bfloat16 [4096, 256], P(('blk', 'rep'))
- grad_weight: float32 [256, 256], replicated
Inputs may be any that keep to these rules, and one draw needn't show every extreme that they name: `tile_col`: the column tiles listed for one block, replica and source block are all different, also in slots at or past the count. `tile_count`: equal to 2 wherever the source block equals the block, and 0 wherever the source block is more than 2 blocks away from the block in both directions around the closed loop of 16 blocks.
All inputs are finite; a program needn't handle non-finite values.
Results may differ from a plain program's by a relative error of at most 0.0049.
Values may be sent and summed in bfloat16 or wider, within the bound.
A program may use at most 64 MiB of HBM per device.

v0:
```python
import jax
import jax.numpy as jnp
from jax import lax
from jax.sharding import PartitionSpec as P


def passed_along(x, axis, by):
    size = lax.axis_size(axis)
    return lax.ppermute(x, axis, [(i, (i + by) % size) for i in range(size)])


def on_device(grad_out, preact, aggregated, weight, degree, neighbors, tile_col, tile_count):
    grad_pre = jnp.where(preact > 0, grad_out, jnp.zeros_like(grad_out))
    local_weight = lax.dot_general(
        aggregated, grad_pre, (((0,), (0,)), ((), ())), preferred_element_type=jnp.float32
    )
    raw_weight = lax.psum(local_weight, ("blk", "rep"))
    norm_value = jnp.sqrt(jnp.sum(raw_weight * raw_weight) + 1e-06)
    grad_weight = raw_weight * jnp.minimum(1.0, 128.0 / norm_value)
    inv_root = 1.0 / jnp.sqrt(degree.astype(jnp.float32))
    backward = lax.dot_general(
        grad_pre, weight, (((1,), (1,)), ((), ())), preferred_element_type=jnp.float32
    )
    scaled = (backward * inv_root[:, None]).astype(jnp.bfloat16)
    listed_all = neighbors[0, 0]
    columns_all = tile_col[0, 0]
    counts_all = tile_count[0, 0]
    slots_total = listed_all.shape[1]
    tile_side = listed_all.shape[3]
    hidden = scaled.shape[1]
    blocks = lax.axis_size("blk")
    replicas = lax.axis_size("rep")
    own_block = lax.axis_index("blk")
    positions = jnp.arange(tile_side, dtype=jnp.int32)
    slot_index = jnp.arange(slots_total, dtype=jnp.int32)

    def absorb(totals, carried, source):
        listed = lax.dynamic_index_in_dim(listed_all, source, 0, keepdims=False)
        column_ids = lax.dynamic_index_in_dim(columns_all, source, 0, keepdims=False)
        present = lax.dynamic_index_in_dim(counts_all, source, 0, keepdims=False)
        adjacency = jnp.sum(
            (listed[:, :, None, :] == positions[None, None, :, None]).astype(jnp.int32), axis=1
        )
        valid = jnp.logical_and(slot_index < present, True).astype(jnp.bfloat16)
        adjacency = adjacency.astype(jnp.bfloat16) * valid[:, None, None]
        contribution = jnp.einsum(
            "sci,if->scf", adjacency, carried, preferred_element_type=jnp.float32
        )
        for slot_number in range(slots_total):
            target = column_ids[slot_number]
            current = lax.dynamic_index_in_dim(totals, target, 0, keepdims=True)
            totals = lax.dynamic_update_index_in_dim(
                totals, current + contribution[slot_number][None], target, 0
            )
        return totals

    empty = jnp.zeros((replicas, tile_side, hidden), jnp.float32)

    def advance(turn, carry):
        sums_now, carried = carry
        carried = passed_along(carried, "blk", 1)
        sums_now = absorb(sums_now, carried, (own_block - turn) % blocks)
        return (sums_now, carried)

    start_sums = absorb(empty, scaled, own_block)
    totals, _ = lax.fori_loop(1, blocks, advance, (start_sums, scaled))
    owned = lax.psum_scatter(totals, "rep", scatter_dimension=0, tiled=True)
    grad_features = (owned[0] * inv_root[:, None]).astype(jnp.bfloat16)
    return (grad_features, grad_weight)


def solution(mesh):
    return jax.shard_map(
        on_device,
        mesh=mesh,
        in_specs=(
            P(("blk", "rep"), None),
            P(("blk", "rep"), None),
            P(("blk", "rep"), None),
            P(),
            P(("blk", "rep")),
            P("blk", "rep", None, None, None, None),
            P("blk", "rep", None, None),
            P("blk", "rep", None),
        ),
        out_specs=(P(("blk", "rep"), None), P()),
        check_vma=False,
    )
```

profile of v0, /device:TPU:0, one launch (start us, length us, event | category | flops | bytes accessed | tf_op | source)
XLA Modules:
  0.0 160.7 jit_solution(10500797936318086954)
XLA Ops:
  8.1 1.8 %convolution_bitcast_fusion = f32[256,256]{0,1:T(8,128)} fusion(bf16[128,256]{1,0:T(8,128)(2,1)} %param.12, bf16[128,256]{1,0:T(8,128)(2,1)} %param.10, bf16[128,256]{1,0:T(8,128)(2,1)} %param.11), kind=kOutput, calls=%fused_computation.16 | convolution fusion | flops 16842752 | bytes 458752 | tf_op jit(solution)/shard_map/dot_general | solution.py:14
  18.0 125.4 %while.18 = (s32[]{:T(128)}, f32[2,128,256]{2,1,0:T(8,128)S(1)}, bf16[128,256]{1,0:T(8,128)(2,1)S(1)}, s32[]{:T(128)}, s32[16,2]{0,1:T(2,128)S(1)}, /*index=5*/s...) while((s32[]{:T(128)}, f32[2,128,256]{2,1,0:T(8,128)S(1)}, ...), condition=%wide.region_3.4_spmd.clone, body=%wide.region_1.0_spmd.clone.sunk | while | flops 17661976 | bytes 1794500 | solution.py:66
  18.1 3.0 %collective-permute-start = (bf16[128,256]{1,0:T(8,128)(2,1)S(1)}, bf16[128,256]{1,0:T(8,128)(2,1)S(1)}, u32[]{:S(2)}, u32[]{:S(2)}) collective-permute-start(bf16[128,256]{1,0:T(8,128)(2,1)S(1)} %get-tuple-element.324), channel_id=1, source_target_pairs={{0,2},{2,4},{4,6},{6,8},{8,10},{10,12},{12,14},{14,16},{16,18},{18... | collective-permute-start | bytes 196616 | tf_op jit(solution)/shard_map/while/body/eval_jaxpr/ppermute | solution.py:9
  24.0 0.7 dynamic-slice_bitcast_fusion.3
  27.6 1.5 collective-permute-start
  36.0 1.3 collective-permute-start
  44.3 1.2 collective-permute-start
  52.5 1.1 collective-permute-start
  60.8 0.9 collective-permute-start
  67.9 0.8 collective-permute-done
  69.0 0.8 collective-permute-start
  76.0 0.9 collective-permute-done
  84.2 1.1 collective-permute-done
  92.3 1.2 collective-permute-done
  100.4 1.3 collective-permute-done
  108.5 1.5 collective-permute-done
  116.7 1.6 collective-permute-done
  124.9 1.6 %collective-permute-done = bf16[128,256]{1,0:T(8,128)(2,1)S(1)} collective-permute-done((bf16[128,256]{1,0:T(8,128)(2,1)S(1)}, bf16[128,256]{1,0:T(8,128)(2,1)S(1)}, u32[]{:S(2)}, u32[]{:S(2)}) %collective-permute-start) | collective-permute-done | bytes 65568 | tf_op jit(solution)/shard_map/while/body/eval_jaxpr/ppermute | solution.py:9
  133.2 1.6 %collective-permute-done = bf16[128,256]{1,0:T(8,128)(2,1)S(1)} collective-permute-done((bf16[128,256]{1,0:T(8,128)(2,1)S(1)}, bf16[128,256]{1,0:T(8,128)(2,1)S(1)}, u32[]{:S(2)}, u32[]{:S(2)}) %collective-permute-start) | collective-permute-done | bytes 65568 | tf_op jit(solution)/shard_map/while/body/eval_jaxpr/ppermute | solution.py:9
  141.5 1.6 %collective-permute-done = bf16[128,256]{1,0:T(8,128)(2,1)S(1)} collective-permute-done((bf16[128,256]{1,0:T(8,128)(2,1)S(1)}, bf16[128,256]{1,0:T(8,128)(2,1)S(1)}, u32[]{:S(2)}, u32[]{:S(2)}) %collective-permute-start) | collective-permute-done | bytes 65568 | tf_op jit(solution)/shard_map/while/body/eval_jaxpr/ppermute | solution.py:9
  144.6 1.7 %multiply_reduce_fusion = f32[]{:T(128)} fusion(f32[256,256]{0,1:T(8,128)} %all-reduce.2.cloned.1.call-done), kind=kLoop, calls=%fused_computation.21 | loop fusion | flops 131071 | bytes 262148 | tf_op jit(solution)/shard_map/reduce_sum | solution.py:18
  147.0 0.8 copy.11
  147.9 3.8 %reduce-scatter.2.cloned.1.call-done = f32[1,128,256]{2,1,0:T(8,128)} async-done(((f32[2,128,256]{2,1,0:T(8,128)}), f32[1,128,256]{2,1,0:T(8,128)}) %reduce-scatter.2.cloned.1.call-update) | async-done | bytes 131088 | tf_op jit(solution)/shard_map/reduce_scatter | solution.py:67
  151.6 1.6 %fusion.13 = bf16[128,256]{1,0:T(8,128)(2,1)} fusion(f32[1,128,256]{2,1,0:T(8,128)} %reduce-scatter.2.cloned.1.call-done, f32[128]{0:T(128)S(1)} %convert_rsqrt_fusion), kind=kLoop, calls=%fused_computation.26 | loop fusion | flops 65536 | bytes 197120 | tf_op jit(solution)/shard_map/convert_element_type | solution.py:68
  (196 shorter events, 53.0 us)
Async XLA Ops:
  8.0 8.9 %copy-start = (bf16[256,256]{1,0:T(8,128)(2,1)S(1)}, bf16[256,256]{1,0:T(8,128)(2,1)}, u32[]{:S(2)}) copy-start(bf16[256,256]{1,0:T(8,128)(2,1)} %param.13) | copy-start | bytes 393220
  8.0 136.6 %all-reduce.2.cloned.1.call-start = ((), (), s32[]{:S(2)}) async-start(), calls=%async_computation.2 | async-start | bytes 524288 | tf_op jit(solution)/shard_map/psum | solution.py:17
  9.9 141.7 %reduce-scatter.2.cloned.1.call-start = ((), (), s32[]{:S(2)}) async-start(), calls=%async_computation.1 | async-start | bytes 393216 | tf_op jit(solution)/shard_map/reduce_scatter | solution.py:67
  10.0 0.7 copy-start.5
  14.4 2.6 %copy-start.3 = (bf16[128,256]{1,0:T(8,128)(2,1)S(1)}, bf16[128,256]{1,0:T(8,128)(2,1)}, u32[]{:S(2)}) copy-start(bf16[128,256]{1,0:T(8,128)(2,1)} %param.10) | copy-start | bytes 196612
  14.4 2.6 %copy-start.4 = (bf16[128,256]{1,0:T(8,128)(2,1)S(1)}, bf16[128,256]{1,0:T(8,128)(2,1)}, u32[]{:S(2)}) copy-start(bf16[128,256]{1,0:T(8,128)(2,1)} %param.11) | copy-start | bytes 196612
  15.6 0.7 copy-start.6
  18.1 9.3 %collective-permute-start = (bf16[128,256]{1,0:T(8,128)(2,1)S(1)}, bf16[128,256]{1,0:T(8,128)(2,1)S(1)}, u32[]{:S(2)}, u32[]{:S(2)}) collective-permute-start(bf16[128,256]{1,0:T(8,128)(2,1)S(1)} %get-tuple-element.324), channel_id=1, source_target_pairs={{0,2},{2,4},{4,6},{6,8},{8,10},{10,12},{12,14},{14,16},{16,18},{18... | collective-permute-start | bytes 196616 | tf_op jit(solution)/shard_map/while/body/eval_jaxpr/ppermute | solution.py:9
  27.6 8.0 %collective-permute-start = (bf16[128,256]{1,0:T(8,128)(2,1)S(1)}, bf16[128,256]{1,0:T(8,128)(2,1)S(1)}, u32[]{:S(2)}, u32[]{:S(2)}) collective-permute-start(bf16[128,256]{1,0:T(8,128)(2,1)S(1)} %get-tuple-element.324), channel_id=1, source_target_pairs={{0,2},{2,4},{4,6},{6,8},{8,10},{10,12},{12,14},{14,16},{16,18},{18... | collective-permute-start | bytes 196616 | tf_op jit(solution)/shard_map/while/body/eval_jaxpr/ppermute | solution.py:9
  36.0 8.0 %collective-permute-start = (bf16[128,256]{1,0:T(8,128)(2,1)S(1)}, bf16[128,256]{1,0:T(8,128)(2,1)S(1)}, u32[]{:S(2)}, u32[]{:S(2)}) collective-permute-start(bf16[128,256]{1,0:T(8,128)(2,1)S(1)} %get-tuple-element.324), channel_id=1, source_target_pairs={{0,2},{2,4},{4,6},{6,8},{8,10},{10,12},{12,14},{14,16},{16,18},{18... | collective-permute-start | bytes 196616 | tf_op jit(solution)/shard_map/while/body/eval_jaxpr/ppermute | solution.py:9
  44.3 7.9 %collective-permute-start = (bf16[128,256]{1,0:T(8,128)(2,1)S(1)}, bf16[128,256]{1,0:T(8,128)(2,1)S(1)}, u32[]{:S(2)}, u32[]{:S(2)}) collective-permute-start(bf16[128,256]{1,0:T(8,128)(2,1)S(1)} %get-tuple-element.324), channel_id=1, source_target_pairs={{0,2},{2,4},{4,6},{6,8},{8,10},{10,12},{12,14},{14,16},{16,18},{18... | collective-permute-start | bytes 196616 | tf_op jit(solution)/shard_map/while/body/eval_jaxpr/ppermute | solution.py:9
  52.5 8.0 %collective-permute-start = (bf16[128,256]{1,0:T(8,128)(2,1)S(1)}, bf16[128,256]{1,0:T(8,128)(2,1)S(1)}, u32[]{:S(2)}, u32[]{:S(2)}) collective-permute-start(bf16[128,256]{1,0:T(8,128)(2,1)S(1)} %get-tuple-element.324), channel_id=1, source_target_pairs={{0,2},{2,4},{4,6},{6,8},{8,10},{10,12},{12,14},{14,16},{16,18},{18... | collective-permute-start | bytes 196616 | tf_op jit(solution)/shard_map/while/body/eval_jaxpr/ppermute | solution.py:9
  60.8 7.9 %collective-permute-start = (bf16[128,256]{1,0:T(8,128)(2,1)S(1)}, bf16[128,256]{1,0:T(8,128)(2,1)S(1)}, u32[]{:S(2)}, u32[]{:S(2)}) collective-permute-start(bf16[128,256]{1,0:T(8,128)(2,1)S(1)} %get-tuple-element.324), channel_id=1, source_target_pairs={{0,2},{2,4},{4,6},{6,8},{8,10},{10,12},{12,14},{14,16},{16,18},{18... | collective-permute-start | bytes 196616 | tf_op jit(solution)/shard_map/while/body/eval_jaxpr/ppermute | solution.py:9
  69.0 8.0 %collective-permute-start = (bf16[128,256]{1,0:T(8,128)(2,1)S(1)}, bf16[128,256]{1,0:T(8,128)(2,1)S(1)}, u32[]{:S(2)}, u32[]{:S(2)}) collective-permute-start(bf16[128,256]{1,0:T(8,128)(2,1)S(1)} %get-tuple-element.324), channel_id=1, source_target_pairs={{0,2},{2,4},{4,6},{6,8},{8,10},{10,12},{12,14},{14,16},{16,18},{18... | collective-permute-start | bytes 196616 | tf_op jit(solution)/shard_map/while/body/eval_jaxpr/ppermute | solution.py:9
  77.3 7.9 %collective-permute-start = (bf16[128,256]{1,0:T(8,128)(2,1)S(1)}, bf16[128,256]{1,0:T(8,128)(2,1)S(1)}, u32[]{:S(2)}, u32[]{:S(2)}) collective-permute-start(bf16[128,256]{1,0:T(8,128)(2,1)S(1)} %get-tuple-element.324), channel_id=1, source_target_pairs={{0,2},{2,4},{4,6},{6,8},{8,10},{10,12},{12,14},{14,16},{16,18},{18... | collective-permute-start | bytes 196616 | tf_op jit(solution)/shard_map/while/body/eval_jaxpr/ppermute | solution.py:9
  85.6 7.9 %collective-permute-start = (bf16[128,256]{1,0:T(8,128)(2,1)S(1)}, bf16[128,256]{1,0:T(8,128)(2,1)S(1)}, u32[]{:S(2)}, u32[]{:S(2)}) collective-permute-start(bf16[128,256]{1,0:T(8,128)(2,1)S(1)} %get-tuple-element.324), channel_id=1, source_target_pairs={{0,2},{2,4},{4,6},{6,8},{8,10},{10,12},{12,14},{14,16},{16,18},{18... | collective-permute-start | bytes 196616 | tf_op jit(solution)/shard_map/while/body/eval_jaxpr/ppermute | solution.py:9
  93.8 7.9 %collective-permute-start = (bf16[128,256]{1,0:T(8,128)(2,1)S(1)}, bf16[128,256]{1,0:T(8,128)(2,1)S(1)}, u32[]{:S(2)}, u32[]{:S(2)}) collective-permute-start(bf16[128,256]{1,0:T(8,128)(2,1)S(1)} %get-tuple-element.324), channel_id=1, source_target_pairs={{0,2},{2,4},{4,6},{6,8},{8,10},{10,12},{12,14},{14,16},{16,18},{18... | collective-permute-start | bytes 196616 | tf_op jit(solution)/shard_map/while/body/eval_jaxpr/ppermute | solution.py:9
  102.1 7.9 %collective-permute-start = (bf16[128,256]{1,0:T(8,128)(2,1)S(1)}, bf16[128,256]{1,0:T(8,128)(2,1)S(1)}, u32[]{:S(2)}, u32[]{:S(2)}) collective-permute-start(bf16[128,256]{1,0:T(8,128)(2,1)S(1)} %get-tuple-element.324), channel_id=1, source_target_pairs={{0,2},{2,4},{4,6},{6,8},{8,10},{10,12},{12,14},{14,16},{16,18},{18... | collective-permute-start | bytes 196616 | tf_op jit(solution)/shard_map/while/body/eval_jaxpr/ppermute | solution.py:9
  110.3 7.9 %collective-permute-start = (bf16[128,256]{1,0:T(8,128)(2,1)S(1)}, bf16[128,256]{1,0:T(8,128)(2,1)S(1)}, u32[]{:S(2)}, u32[]{:S(2)}) collective-permute-start(bf16[128,256]{1,0:T(8,128)(2,1)S(1)} %get-tuple-element.324), channel_id=1, source_target_pairs={{0,2},{2,4},{4,6},{6,8},{8,10},{10,12},{12,14},{14,16},{16,18},{18... | collective-permute-start | bytes 196616 | tf_op jit(solution)/shard_map/while/body/eval_jaxpr/ppermute | solution.py:9
  118.6 8.0 %collective-permute-start = (bf16[128,256]{1,0:T(8,128)(2,1)S(1)}, bf16[128,256]{1,0:T(8,128)(2,1)S(1)}, u32[]{:S(2)}, u32[]{:S(2)}) collective-permute-start(bf16[128,256]{1,0:T(8,128)(2,1)S(1)} %get-tuple-element.324), channel_id=1, source_target_pairs={{0,2},{2,4},{4,6},{6,8},{8,10},{10,12},{12,14},{14,16},{16,18},{18... | collective-permute-start | bytes 196616 | tf_op jit(solution)/shard_map/while/body/eval_jaxpr/ppermute | solution.py:9
  126.9 8.0 %collective-permute-start = (bf16[128,256]{1,0:T(8,128)(2,1)S(1)}, bf16[128,256]{1,0:T(8,128)(2,1)S(1)}, u32[]{:S(2)}, u32[]{:S(2)}) collective-permute-start(bf16[128,256]{1,0:T(8,128)(2,1)S(1)} %get-tuple-element.324), channel_id=1, source_target_pairs={{0,2},{2,4},{4,6},{6,8},{8,10},{10,12},{12,14},{14,16},{16,18},{18... | collective-permute-start | bytes 196616 | tf_op jit(solution)/shard_map/while/body/eval_jaxpr/ppermute | solution.py:9
  135.2 8.0 %collective-permute-start = (bf16[128,256]{1,0:T(8,128)(2,1)S(1)}, bf16[128,256]{1,0:T(8,128)(2,1)S(1)}, u32[]{:S(2)}, u32[]{:S(2)}) collective-permute-start(bf16[128,256]{1,0:T(8,128)(2,1)S(1)} %get-tuple-element.324), channel_id=1, source_target_pairs={{0,2},{2,4},{4,6},{6,8},{8,10},{10,12},{12,14},{14,16},{16,18},{18... | collective-permute-start | bytes 196616 | tf_op jit(solution)/shard_map/while/body/eval_jaxpr/ppermute | solution.py:9
  143.5 0.7 copy-start.1
  144.6 2.4 %copy-start.2 = (f32[256,256]{0,1:T(8,128)S(1)}, f32[256,256]{0,1:T(8,128)}, u32[]{:S(2)}) copy-start(f32[256,256]{0,1:T(8,128)} %all-reduce.2.cloned.1.call-done) | copy-start | bytes 786436
  (1 other events, 0.7 us)
Sparse Core Ops, SparseCore 0:
  15.8 128.7 all-reduce.1
Sparse Core Ops, SparseCore 1:
  144.3 7.3 reduce-scatter.1
where the time goes:
time: 163 us; the launch traced here: 161 us
  loops' own time  54.4 us (33%)
  local copies, waits for them, and re-layouts  33.7 us (21%)
  between operations  19.9 us (12%)
  waiting for transfers between devices  19.2 us (12%)
  other arithmetic  16 us (10%)
  starting transfers between devices  11.8 us (7%)
  matrix products  5.65 us (3%)
    another operation x1, loops' own time, on_device(): totals, _ = lax.fori_loop(1, blocks, advance, (start_sums, scaled))  54.4 us
    ppermute x15, waiting for transfers between devices, passed_along(): return lax.ppermute(x, axis, [(i, (i + by) % size) for i in range(size)])  15 us
    ppermute x15, starting transfers between devices, passed_along(): return lax.ppermute(x, axis, [(i, (i + by) % size) for i in range(size)])  11.7 us
    eq x16, local copies, waits for them, and re-layouts, absorb(): listed[:, :, None, :] == positions[None, None, :, None]  11.3 us
    convert_element_type x16, other arithmetic, absorb(): valid = jnp.logical_and(slot_index < present, True).astype(jnp.bfloat16)  10.1 us
    dynamic_slice x16, local copies, waits for them, and re-layouts, absorb(): present = lax.dynamic_index_in_dim(counts_all, source, 0, keepdims=False)  9.95 us
    slice x16, local copies, waits for them, and re-layouts, absorb(): target = column_ids[slot_number]  8.47 us
    reduce_scatter x1, waiting for transfers between devices, on_device(): owned = lax.psum_scatter(totals, 'rep', scatter_dimension=0, tiled=True)  3.76 us
  transfers between devices with their start and end apart: 17, of which 16 were waited for; matrix products, arithmetic and copies ran while one was open for 31% of the time, Pallas kernels for 0%

commit v1 on v0

v1 whole, which is shorter than its diff:
```python
import functools

import jax
import jax.numpy as jnp
from jax import lax
from jax.experimental import pallas as pl
from jax.experimental.pallas import tpu as pltpu
from jax.sharding import PartitionSpec as P

MESH = pl.DeviceIdType.MESH
REACH = 2
LANES = 128
PACKED_ROWS = 16


def kernel(
    blocks,
    replicas,
    members,
    offsets,
    grad_out_hbm,
    preact_hbm,
    aggregated_hbm,
    weight_hbm,
    degree_ref,
    neighbors_hbm,
    column_ref,
    count_ref,
    features_ref,
    weight_out_ref,
    grad_out_ref,
    preact_ref,
    aggregated_ref,
    weight_ref,
    listed_ref,
    local_ref,
    part_ref,
    spread_ref,
    across_ref,
    gathered_ref,
    rows_ref,
    tiles_ref,
    partial_ref,
    landed_ref,
    load_sem,
    spread_sem,
    across_sem,
    gather_sem,
    rows_send_sem,
    rows_recv_sem,
    partial_send_sem,
    partial_recv_sem,
):
    block, replica = lax.axis_index("blk"), lax.axis_index("rep")
    me = block * replicas + replica
    groups = blocks * replicas // members
    group, member = me // members, lax.rem(me, members)
    tile_side, hidden = grad_out_ref.shape
    slots = listed_ref.shape[1]
    depth = listed_ref.shape[2]
    piece = part_ref.shape[0] // members
    halves = hidden // LANES

    def device(flat):
        return (flat // replicas, lax.rem(flat, replicas))

    def group_peer(step):
        return group * members + lax.rem(member + step, members)

    def across_peer(step):
        return lax.rem(group + step, groups) * members + member

    def near_device(offset):
        return (lax.rem(block + offset + blocks, blocks), replica)

    def replica_device(step):
        return (block, lax.rem(replica + step, replicas))

    def piece_rows(index):
        return pl.ds(pl.multiple_of(index * piece, piece), piece)

    barrier = pltpu.get_barrier_semaphore()

    def greet(target):
        pl.semaphore_signal(barrier, inc=1, device_id=target, device_id_type=MESH)

    def greet_member(step, carry):
        greet(device(group_peer(step)))
        return carry

    lax.fori_loop(1, members, greet_member, 0)
    greeted = members - 1
    if groups > 1:
        for step in range(1, groups):
            greet(device(across_peer(step)))
        for offset in offsets:
            greet(near_device(offset))
        for step in range(1, replicas):
            greet(replica_device(step))
        greeted += groups - 1 + len(offsets) + replicas - 1

    loads = [
        pltpu.make_async_copy(source, target, load_sem.at[index])
        for index, (source, target) in enumerate(
            (
                (grad_out_hbm, grad_out_ref),
                (preact_hbm, preact_ref),
                (aggregated_hbm, aggregated_ref),
                (weight_hbm, weight_ref),
            )
        )
    ]
    sources = [block] + [lax.rem(block - offset + blocks, blocks) for offset in offsets]
    for index, source in enumerate(sources):
        loads.append(
            pltpu.make_async_copy(
                neighbors_hbm.at[0, 0, source], listed_ref.at[index], load_sem.at[4 + index]
            )
        )
    for load in loads:
        load.start()

    inverse = 1.0 / jnp.sqrt(degree_ref[...].astype(jnp.float32))
    inverse = jnp.transpose(jnp.broadcast_to(inverse, (tile_side, tile_side)))[:, :1]

    loads[0].wait()
    loads[1].wait()
    loads[2].wait()
    grad_pre = jnp.where(
        preact_ref[...].astype(jnp.float32) > 0, grad_out_ref[...].astype(jnp.float32), 0.0
    ).astype(jnp.bfloat16)
    local = lax.dot_general(
        aggregated_ref[...], grad_pre, (((0,), (0,)), ((), ())), preferred_element_type=jnp.float32
    )
    for half in range(halves):
        rows = pl.ds(half * hidden, hidden)
        columns = local[:, half * LANES : (half + 1) * LANES]
        local_ref[rows] = columns
        part_ref[rows] = columns.astype(jnp.bfloat16)
    loads[3].wait()
    backward = lax.dot_general(
        grad_pre, weight_ref[...], (((1,), (1,)), ((), ())), preferred_element_type=jnp.float32
    )
    rows_ref[pl.ds(0, tile_side)] = (backward * inverse).astype(jnp.bfloat16)

    pl.semaphore_wait(barrier, greeted)

    def send_piece(step, carry):
        peer = group_peer(step)
        pltpu.make_async_remote_copy(
            src_ref=part_ref.at[piece_rows(lax.rem(peer, members))],
            dst_ref=spread_ref.at[piece_rows(step - 1)],
            send_sem=spread_sem.at[0],
            recv_sem=spread_sem.at[1],
            device_id=device(peer),
            device_id_type=MESH,
        ).start()
        return carry

    lax.fori_loop(1, members, send_piece, 0)

    row_copies = []
    for index, offset in enumerate(offsets):
        copy = pltpu.make_async_remote_copy(
            src_ref=rows_ref.at[pl.ds(0, tile_side)],
            dst_ref=rows_ref.at[pl.ds((index + 1) * tile_side, tile_side)],
            send_sem=rows_send_sem.at[index],
            recv_sem=rows_recv_sem.at[index],
            device_id=near_device(offset),
            device_id_type=MESH,
        )
        copy.start()
        row_copies.append(copy)

    positions = lax.broadcasted_iota(jnp.int32, (tile_side, tile_side), 0)
    for index, source in enumerate(sources):
        loads[4 + index].wait()
        totals = [jnp.zeros((tile_side, tile_side), jnp.float32) for _ in range(replicas)]
        for slot in range(slots):
            counted = jnp.zeros((tile_side, tile_side), jnp.float32)
            for entry in range(depth):
                listed = listed_ref[index, slot, pl.ds(entry, 1), :]
                counted += jnp.where(listed == positions, 1.0, 0.0)
            column = column_ref[0, 0, slot, source]
            present = slot < count_ref[0, 0, source]
            for step in range(replicas):
                here = jnp.logical_and(present, column == lax.rem(replica + step, replicas))
                totals[step] += counted * jnp.where(here, 1.0, 0.0)
        for step in range(replicas):
            tiles_ref[
                pl.ds(step * tile_side, tile_side), pl.ds(index * tile_side, tile_side)
            ] = totals[step].astype(jnp.bfloat16)

    def product(first_row, row_count, first_source, source_count):
        return jnp.dot(
            tiles_ref[
                pl.ds(first_row * tile_side, row_count * tile_side),
                pl.ds(first_source * tile_side, source_count * tile_side),
            ],
            rows_ref[pl.ds(first_source * tile_side, source_count * tile_side)],
            preferred_element_type=jnp.float32,
        )

    def wait_all(ref, sem, count):
        rows = ref.at[pl.ds(0, count * piece)]
        pltpu.make_async_copy(rows, rows, sem).wait()

    wait_all(spread_ref, spread_sem.at[1], members - 1)
    reduced = local_ref[piece_rows(member)]
    for step in range(members - 1):
        reduced += spread_ref[pl.ds(step * piece, piece)].astype(jnp.float32)

    if groups > 1:
        across_ref[0] = reduced
        across_copies = []
        for step in range(1, groups):
            copy = pltpu.make_async_remote_copy(
                src_ref=across_ref.at[0],
                dst_ref=across_ref.at[step],
                send_sem=across_sem.at[0, step],
                recv_sem=across_sem.at[1, step],
                device_id=device(across_peer(step)),
                device_id_type=MESH,
            )
            copy.start()
            across_copies.append(copy)
        for step in range(1, groups):
            across_copies[step - 1].wait()
            reduced += across_ref[step]

    gathered_ref[piece_rows(member)] = reduced.astype(jnp.bfloat16)

    def send_reduced(step, carry):
        pltpu.make_async_remote_copy(
            src_ref=gathered_ref.at[piece_rows(member)],
            dst_ref=gathered_ref.at[piece_rows(member)],
            send_sem=gather_sem.at[0],
            recv_sem=gather_sem.at[1],
            device_id=device(group_peer(step)),
            device_id_type=MESH,
        ).start()
        return carry

    lax.fori_loop(1, members, send_reduced, 0)

    for copy in row_copies:
        copy.wait_recv()
    partial_copies = []
    if replicas > 1:
        partial_ref[...] = product(1, replicas - 1, 0, len(sources))
        for step in range(1, replicas):
            copy = pltpu.make_async_remote_copy(
                src_ref=partial_ref.at[pl.ds((step - 1) * tile_side, tile_side)],
                dst_ref=landed_ref.at[pl.ds((step - 1) * tile_side, tile_side)],
                send_sem=partial_send_sem.at[step - 1],
                recv_sem=partial_recv_sem.at[step - 1],
                device_id=replica_device(step),
                device_id_type=MESH,
            )
            copy.start()
            partial_copies.append(copy)
    owned = product(0, 1, 0, len(sources))
    for step, copy in enumerate(partial_copies):
        copy.wait_recv()
        owned += landed_ref[pl.ds(step * tile_side, tile_side)]
    features_ref[...] = (owned * inverse).astype(jnp.bfloat16)

    wait_all(gathered_ref, gather_sem.at[1], members - 1)
    raw = gathered_ref[...].astype(jnp.float32)
    total = jnp.sum(jnp.sum(raw * raw, axis=0, keepdims=True), axis=1, keepdims=True)
    scale = jnp.minimum(1.0, 128.0 / jnp.sqrt(total + 1e-06))
    for half in range(halves):
        weight_out_ref[:, pl.ds(half * LANES, LANES)] = (
            raw[half * hidden : (half + 1) * hidden] * scale
        )

    wait_all(spread_ref, spread_sem.at[0], members - 1)
    wait_all(gathered_ref, gather_sem.at[0], members - 1)
    for copy in row_copies + partial_copies:
        copy.wait_send()


def on_device(
    blocks, replicas, grad_out, preact, aggregated, weight, degree, neighbors, tile_col, tile_count
):
    tile_side, hidden = grad_out.shape
    slots, depth = neighbors.shape[3], neighbors.shape[4]
    packed = hidden * hidden // LANES
    members = min(blocks * replicas, packed // PACKED_ROWS)
    groups = blocks * replicas // members
    piece = packed // members
    offsets = []
    for distance in range(1, REACH + 1):
        for offset in (distance, -distance):
            if offset % blocks and offset % blocks not in [o % blocks for o in offsets]:
                offsets.append(offset)
    near = len(offsets) + 1
    others = max(replicas - 1, 1)
    hbm = pl.BlockSpec(memory_space=pltpu.HBM)
    vmem = pl.BlockSpec(memory_space=pltpu.VMEM)
    smem = pl.BlockSpec(memory_space=pltpu.SMEM)
    return pl.pallas_call(
        functools.partial(kernel, blocks, replicas, members, tuple(offsets)),
        out_shape=(
            jax.ShapeDtypeStruct((tile_side, hidden), jnp.bfloat16),
            jax.ShapeDtypeStruct((hidden, hidden), jnp.float32),
        ),
        in_specs=[hbm, hbm, hbm, hbm, vmem, hbm, smem, smem],
        out_specs=(vmem, vmem),
        scratch_shapes=[
            pltpu.VMEM((tile_side, hidden), jnp.bfloat16),
            pltpu.VMEM((tile_side, hidden), jnp.bfloat16),
            pltpu.VMEM((tile_side, hidden), jnp.bfloat16),
            pltpu.VMEM((hidden, hidden), jnp.bfloat16),
            pltpu.VMEM((near, slots, depth, tile_side), jnp.int32),
            pltpu.VMEM((packed, LANES), jnp.float32),
            pltpu.VMEM((packed, LANES), jnp.bfloat16),
            pltpu.VMEM((packed, LANES), jnp.bfloat16),
            pltpu.VMEM((groups, piece, LANES), jnp.float32),
            pltpu.VMEM((packed, LANES), jnp.bfloat16),
            pltpu.VMEM((near * tile_side, hidden), jnp.bfloat16),
            pltpu.VMEM((replicas * tile_side, near * tile_side), jnp.bfloat16),
            pltpu.VMEM((others * tile_side, hidden), jnp.float32),
            pltpu.VMEM((others * tile_side, hidden), jnp.float32),
            pltpu.SemaphoreType.DMA((4 + near,)),
            pltpu.SemaphoreType.DMA((2,)),
            pltpu.SemaphoreType.DMA((2, groups)),
            pltpu.SemaphoreType.DMA((2,)),
            pltpu.SemaphoreType.DMA((near,)),
            pltpu.SemaphoreType.DMA((near,)),
            pltpu.SemaphoreType.DMA((others,)),
            pltpu.SemaphoreType.DMA((others,)),
        ],
        compiler_params=pltpu.CompilerParams(
            collective_id=0, has_side_effects=True, vmem_limit_bytes=32 * 1024 * 1024
        ),
    )(
        grad_out,
        preact,
        aggregated,
        weight,
        degree.reshape(1, tile_side),
        neighbors,
        jnp.swapaxes(tile_col, 2, 3),
        tile_count,
    )


def solution(mesh):
    return jax.shard_map(
        functools.partial(on_device, mesh.shape["blk"], mesh.shape["rep"]),
        mesh=mesh,
        in_specs=(
            P(("blk", "rep"), None),
            P(("blk", "rep"), None),
            P(("blk", "rep"), None),
            P(),
            P(("blk", "rep")),
            P("blk", "rep", None, None, None, None),
            P("blk", "rep", None, None),
            P("blk", "rep", None),
        ),
        out_specs=(P(("blk", "rep"), None), P()),
        check_vma=False,
    )
```

time: 163 us -> 26.6 us (0.16); the launches traced: 161 us -> 26.3 us
  loops' own time: 54.4 us -> 0 us
  local copies, waits for them, and re-layouts: 33.7 us -> 6.33 us
  Pallas kernels: 0 us -> 19.3 us
  between operations: 19.9 us -> 0.67 us
  waiting for transfers between devices: 19.2 us -> 0 us
  other arithmetic: 16 us -> 0 us
  starting transfers between devices: 11.8 us -> 0 us
  matrix products: 5.65 us -> 0 us
    another operation x1 -> x0, loops' own time: 54.4 us -> none  [on_device(): totals, _ = lax.fori_loop(1, blocks, advance, (start_sums, scaled))]
    pallas_call x0 -> x1, Pallas kernels: none -> 19.3 us  [on_device(): pl.pallas_call(functools.partial(kernel, blocks, replicas, members, tuple...]
    ppermute x15 -> x0, waiting for transfers between devices: 15 us -> none  [passed_along(): return lax.ppermute(x, axis, [(i, (i + by) % size) for i in range(size)])]
    convert_element_type x17 -> x0, other arithmetic: 11.7 us -> none  [the longest x16 10.1 us: absorb(): valid = jnp.logical_and(slot_index < present, True).astype(jnp.bfloat16)]
    ppermute x15 -> x0, starting transfers between devices: 11.7 us -> none  [passed_along(): return lax.ppermute(x, axis, [(i, (i + by) % size) for i in range(size)])]
    eq x16 -> x0, local copies, waits for them, and re-layouts: 11.3 us -> none  [absorb(): listed[:, :, None, :] == positions[None, None, :, None]]
    dynamic_slice x32 -> x0, local copies, waits for them, and re-layouts: 11.1 us -> none  [the longest x16 9.95 us: absorb(): present = lax.dynamic_index_in_dim(counts_all, source, 0, keepdims=False)]
    slice x16 -> x0, local copies, waits for them, and re-layouts: 8.47 us -> none  [absorb(): target = column_ids[slot_number]]
  transfers between devices with their start and end apart: 17 -> 0, of which waited for: 16 -> 0; matrix products, arithmetic and copies ran while one was open for 31% -> 0% of each run, Pallas kernels for 0% -> 0%
where the time goes in v1:
time: 26.6 us; the launch traced here: 26.3 us
  Pallas kernels  19.3 us (73%)
  local copies, waits for them, and re-layouts  6.33 us (24%)
  between operations  0.67 us (3%)
    pallas_call x1, Pallas kernels, on_device(): pl.pallas_call(functools.partial(kernel, blocks, replicas, members, tuple...  19.3 us
    unnamed x18, local copies, waits for them, and re-layouts  6.33 us

profile of v1, /device:TPU:0, one launch (start us, length us, event | category | flops | bytes accessed | tf_op | source)
XLA Modules:
  0.0 26.3 jit_solution(1894172668413521212)
XLA Ops:
  0.6 0.0 copy-start.7
  0.6 0.0 copy-start.5
  0.7 0.0 copy-start.6
  0.7 0.6 %copy-done.7 = s32[1,1,16]{2,1,0:T(1,128)S(1)} copy-done((s32[1,1,16]{2,1,0:T(1,128)S(1)}, s32[1,1,16]{2,1,0:T(1,128)}, u32[]{:S(2)}) %copy-start.7) | copy-done | bytes 88
  1.3 0.0 copy-done.5
  1.3 0.0 copy-done.6
  1.3 0.0 copy-start
  1.3 0.9 %copy-done = bf16[256,256]{1,0:T(8,128)(2,1)S(1)} copy-done((bf16[256,256]{1,0:T(8,128)(2,1)S(1)}, bf16[256,256]{1,0:T(8,128)(2,1)}, u32[]{:S(2)}) %copy-start) | copy-done | bytes 131096
  2.2 0.0 copy-start.1
  2.2 0.9 %copy-done.1 = s32[1,1,16,2,8,128]{5,4,3,2,1,0:T(8,128)S(1)} copy-done((s32[1,1,16,2,8,128]{5,4,3,2,1,0:T(8,128)S(1)}, s32[1,1,16,2,8,128]{5,4,3,2,1,0:T(8,128)}, u32[]{:S(2)}) %copy-start.1) | copy-done | bytes 131096
  3.1 0.0 copy-start.2
  3.1 0.8 %copy-done.2 = bf16[128,256]{1,0:T(8,128)(2,1)S(1)} copy-done((bf16[128,256]{1,0:T(8,128)(2,1)S(1)}, bf16[128,256]{1,0:T(8,128)(2,1)}, u32[]{:S(2)}) %copy-start.2) | copy-done | bytes 65560
  4.0 0.0 copy-start.3
  4.0 0.8 %copy-done.3 = bf16[128,256]{1,0:T(8,128)(2,1)S(1)} copy-done((bf16[128,256]{1,0:T(8,128)(2,1)S(1)}, bf16[128,256]{1,0:T(8,128)(2,1)}, u32[]{:S(2)}) %copy-start.3) | copy-done | bytes 65560
  4.8 0.0 copy-start.4
  4.8 0.8 %copy-done.4 = bf16[128,256]{1,0:T(8,128)(2,1)S(1)} copy-done((bf16[128,256]{1,0:T(8,128)(2,1)S(1)}, bf16[128,256]{1,0:T(8,128)(2,1)}, u32[]{:S(2)}) %copy-start.4) | copy-done | bytes 65560
  5.7 19.3 %shard_map.95 = (bf16[128,256]{1,0:T(8,128)(2,1)S(1)}, f32[256,256]{1,0:T(8,128)S(1)}) custom-call(bf16[128,256]{1,0:T(8,128)(2,1)S(1)} %copy-done.2, bf16[128,256]{1,0:T(8,128)(2,1)S(1)} %copy-done.3, bf16[128,256]{1,0:T(8,128)(2,1)S(1)} %copy-done.4, bf16[256,256]{1,0:T(8,128)(2,1)S(1)} %copy-done, s32[1,128]{1,0:T(1,128)S(1)} %bitcast.3, ...), custom_call_target="tpu_custom_call" | custom-call | tf_op jit(solution)/shard_map/pallas_call | solution.py:302
  25.0 0.6 %copy.12 = bf16[128,256]{1,0:T(8,128)(2,1)} copy(bf16[128,256]{1,0:T(8,128)(2,1)S(1)} %get-tuple-element.4) | data formatting | bytes 131072
  25.6 0.7 %copy.13 = f32[256,256]{1,0:T(8,128)} copy(f32[256,256]{1,0:T(8,128)S(1)} %get-tuple-element.5) | data formatting | bytes 524288
Async XLA Ops:
  0.6 0.7 %copy-start.7 = (s32[1,1,16]{2,1,0:T(1,128)S(1)}, s32[1,1,16]{2,1,0:T(1,128)}, u32[]{:S(2)}) copy-start(s32[1,1,16]{2,1,0:T(1,128)} %count_ref.1) | copy-start | bytes 196
  0.6 0.7 %copy-start.5 = (s32[1,1,16,2]{2,3,1,0:T(2,128)S(1)}, s32[1,1,16,2]{2,3,1,0:T(2,128)}, u32[]{:S(2)}) copy-start(s32[1,1,16,2]{2,3,1,0:T(2,128)} %param.14) | copy-start | bytes 388
  0.7 0.7 %copy-start.6 = (s32[128]{0:T(128)S(1)}, s32[128]{0:T(128)}, u32[]{:S(2)}) copy-start(s32[128]{0:T(128)} %param.12) | copy-start | bytes 1540
  1.3 0.9 %copy-start = (bf16[256,256]{1,0:T(8,128)(2,1)S(1)}, bf16[256,256]{1,0:T(8,128)(2,1)}, u32[]{:S(2)}) copy-start(bf16[256,256]{1,0:T(8,128)(2,1)} %weight_hbm.1) | copy-start | bytes 393220
  2.2 0.9 %copy-start.1 = (s32[1,1,16,2,8,128]{5,4,3,2,1,0:T(8,128)S(1)}, s32[1,1,16,2,8,128]{5,4,3,2,1,0:T(8,128)}, u32[]{:S(2)}) copy-start(s32[1,1,16,2,8,128]{5,4,3,2,1,0:T(8,128)} %neighbors_hbm.1) | copy-start | bytes 393220
  3.1 0.8 %copy-start.2 = (bf16[128,256]{1,0:T(8,128)(2,1)S(1)}, bf16[128,256]{1,0:T(8,128)(2,1)}, u32[]{:S(2)}) copy-start(bf16[128,256]{1,0:T(8,128)(2,1)} %grad_out_hbm.1) | copy-start | bytes 196612
  4.0 0.8 %copy-start.3 = (bf16[128,256]{1,0:T(8,128)(2,1)S(1)}, bf16[128,256]{1,0:T(8,128)(2,1)}, u32[]{:S(2)}) copy-start(bf16[128,256]{1,0:T(8,128)(2,1)} %preact_hbm.1) | copy-start | bytes 196612
  4.8 0.8 %copy-start.4 = (bf16[128,256]{1,0:T(8,128)(2,1)S(1)}, bf16[128,256]{1,0:T(8,128)(2,1)}, u32[]{:S(2)}) copy-start(bf16[128,256]{1,0:T(8,128)(2,1)} %aggregated_hbm.1) | copy-start | bytes 196612

commit v2 on v1

--- a/solution.py
+++ b/solution.py
@@ -332,7 +332,7 @@
             pltpu.SemaphoreType.DMA((others,)),
         ],
         compiler_params=pltpu.CompilerParams(
-            collective_id=0, has_side_effects=True, vmem_limit_bytes=32 * 1024 * 1024
+            collective_id=0, has_side_effects=True, vmem_limit_bytes=63 * 1024 * 1024
         ),
     )(
         grad_out,

time: 26.6 us -> 24.3 us (0.914)
  local copies, waits for them, and re-layouts: 6.33 us -> 3.14 us
  Pallas kernels: 19.3 us -> 20.3 us
    unnamed x18 -> x2, local copies, waits for them, and re-layouts: 6.33 us -> 3.14 us
    pallas_call x1, Pallas kernels: 19.3 us -> 20.3 us  [on_device(): pl.pallas_call(functools.partial(kernel, blocks, replicas, members, tuple...]
where the time goes in v2:
time: 24.3 us; the launch traced here: 24.1 us
  Pallas kernels  20.3 us (84%)
  local copies, waits for them, and re-layouts  3.14 us (13%)
  between operations  0.64 us (3%)
    pallas_call x1, Pallas kernels, on_device(): pl.pallas_call(functools.partial(kernel, blocks, replicas, members, tuple...  20.3 us
    unnamed x2, local copies, waits for them, and re-layouts  3.14 us

profile of v2, /device:TPU:0, one launch (start us, length us, event | category | flops | bytes accessed | tf_op | source)
XLA Modules:
  0.0 24.1 jit_solution(12830222690510688236)
XLA Ops:
  0.6 20.3 %shard_map.95 = (bf16[128,256]{1,0:T(8,128)(2,1)}, f32[256,256]{1,0:T(8,128)}) custom-call(bf16[128,256]{1,0:T(8,128)(2,1)} %grad_out_hbm.1, bf16[128,256]{1,0:T(8,128)(2,1)} %preact_hbm.1, bf16[128,256]{1,0:T(8,128)(2,1)} %aggregated_hbm.1, bf16[256,256]{1,0:T(8,128)(2,1)} %weight_hbm.1, s32[1,128]{1,0:T(1,128)} %bitcast.3, ...), custom_call_target="tpu_custom_call" | custom-call | tf_op jit(solution)/shard_map/pallas_call | solution.py:302
  20.9 1.5 %copy.12 = bf16[128,256]{1,0:T(8,128)(2,1)} copy(bf16[128,256]{1,0:T(8,128)(2,1)} %get-tuple-element.4) | data formatting | bytes 131072
  22.4 1.7 %copy.13 = f32[256,256]{1,0:T(8,128)} copy(f32[256,256]{1,0:T(8,128)} %get-tuple-element.5) | data formatting | bytes 524288

commit v3 on v2

--- a/solution.py
+++ b/solution.py
@@ -34,6 +34,8 @@
     weight_ref,
     listed_ref,
     local_ref,
+    shared_ref,
+    mine_ref,
     part_ref,
     spread_ref,
     across_ref,
@@ -43,32 +45,33 @@
     partial_ref,
     landed_ref,
     load_sem,
+    shared_send_sem,
+    shared_recv_sem,
     spread_sem,
     across_sem,
     gather_sem,
+    share_send_sem,
+    share_recv_sem,
     rows_send_sem,
     rows_recv_sem,
     partial_send_sem,
     partial_recv_sem,
 ):
     block, replica = lax.axis_index("blk"), lax.axis_index("rep")
-    me = block * replicas + replica
-    groups = blocks * replicas // members
-    group, member = me // members, lax.rem(me, members)
+    groups = blocks // members
+    group, member = block // members, lax.rem(block, members)
     tile_side, hidden = grad_out_ref.shape
     slots = listed_ref.shape[1]
     depth = listed_ref.shape[2]
-    piece = part_ref.shape[0] // members
+    share = part_ref.shape[0]
+    piece = share // members
     halves = hidden // LANES
 
-    def device(flat):
-        return (flat // replicas, lax.rem(flat, replicas))
-
-    def group_peer(step):
-        return group * members + lax.rem(member + step, members)
-
-    def across_peer(step):
-        return lax.rem(group + step, groups) * members + member
+    def member_device(step):
+        return (group * members + lax.rem(member + step, members), replica)
+
+    def across_device(step):
+        return (lax.rem(group + step, groups) * members + member, replica)
 
     def near_device(offset):
         return (lax.rem(block + offset + blocks, blocks), replica)
@@ -79,25 +82,17 @@
     def piece_rows(index):
         return pl.ds(pl.multiple_of(index * piece, piece), piece)
 
+    def share_rows(index):
+        return pl.ds(pl.multiple_of(index * share, share), share)
+
     barrier = pltpu.get_barrier_semaphore()
-
-    def greet(target):
+    greeted = [replica_device(step) for step in range(1, replicas)]
+    greeted += [member_device(step) for step in range(1, members)]
+    if groups > 1:
+        greeted += [across_device(step) for step in range(1, groups)]
+        greeted += [near_device(offset) for offset in offsets]
+    for target in greeted:
         pl.semaphore_signal(barrier, inc=1, device_id=target, device_id_type=MESH)
-
-    def greet_member(step, carry):
-        greet(device(group_peer(step)))
-        return carry
-
-    lax.fori_loop(1, members, greet_member, 0)
-    greeted = members - 1
-    if groups > 1:
-        for step in range(1, groups):
-            greet(device(across_peer(step)))
-        for offset in offsets:
-            greet(near_device(offset))
-        for step in range(1, replicas):
-            greet(replica_device(step))
-        greeted += groups - 1 + len(offsets) + replicas - 1
 
     loads = [
         pltpu.make_async_copy(source, target, load_sem.at[index])
@@ -136,44 +131,49 @@
         rows = pl.ds(half * hidden, hidden)
         columns = local[:, half * LANES : (half + 1) * LANES]
         local_ref[rows] = columns
-        part_ref[rows] = columns.astype(jnp.bfloat16)
     loads[3].wait()
     backward = lax.dot_general(
         grad_pre, weight_ref[...], (((1,), (1,)), ((), ())), preferred_element_type=jnp.float32
     )
     rows_ref[pl.ds(0, tile_side)] = (backward * inverse).astype(jnp.bfloat16)
 
-    pl.semaphore_wait(barrier, greeted)
-
-    def send_piece(step, carry):
-        peer = group_peer(step)
-        pltpu.make_async_remote_copy(
-            src_ref=part_ref.at[piece_rows(lax.rem(peer, members))],
-            dst_ref=spread_ref.at[piece_rows(step - 1)],
-            send_sem=spread_sem.at[0],
-            recv_sem=spread_sem.at[1],
-            device_id=device(peer),
+    pl.semaphore_wait(barrier, len(greeted))
+
+    shared_copies = []
+    for step in range(1, replicas):
+        copy = pltpu.make_async_remote_copy(
+            src_ref=local_ref.at[share_rows(lax.rem(replica + step, replicas))],
+            dst_ref=shared_ref.at[pl.ds((step - 1) * share, share)],
+            send_sem=shared_send_sem.at[step - 1],
+            recv_sem=shared_recv_sem.at[step - 1],
+            device_id=replica_device(step),
             device_id_type=MESH,
-        ).start()
-        return carry
-
-    lax.fori_loop(1, members, send_piece, 0)
+        )
+        copy.start()
+        shared_copies.append(copy)
 
     row_copies = []
-    for index, offset in enumerate(offsets):
+
+    def send_rows(index):
         copy = pltpu.make_async_remote_copy(
             src_ref=rows_ref.at[pl.ds(0, tile_side)],
             dst_ref=rows_ref.at[pl.ds((index + 1) * tile_side, tile_side)],
             send_sem=rows_send_sem.at[index],
             recv_sem=rows_recv_sem.at[index],
-            device_id=near_device(offset),
+            device_id=near_device(offsets[index]),
             device_id_type=MESH,
         )
         copy.start()
         row_copies.append(copy)
 
+    early = len(offsets) // 2
+    for index in range(early):
+        send_rows(index)
+
     positions = lax.broadcasted_iota(jnp.int32, (tile_side, tile_side), 0)
-    for index, source in enumerate(sources):
+
+    def build_tiles(index):
+        source = sources[index]
         loads[4 + index].wait()
         totals = [jnp.zeros((tile_side, tile_side), jnp.float32) for _ in range(replicas)]
         for slot in range(slots):
@@ -205,8 +205,31 @@
         rows = ref.at[pl.ds(0, count * piece)]
         pltpu.make_async_copy(rows, rows, sem).wait()
 
+    for index in range(2):
+        build_tiles(index)
+
+    mine = local_ref[share_rows(replica)]
+    for step, copy in enumerate(shared_copies):
+        copy.wait_recv()
+        mine += shared_ref[pl.ds(step * share, share)]
+    mine_ref[...] = mine
+    part_ref[...] = mine.astype(jnp.bfloat16)
+    for step in range(1, members):
+        pltpu.make_async_remote_copy(
+            src_ref=part_ref.at[piece_rows(lax.rem(member + step, members))],
+            dst_ref=spread_ref.at[piece_rows(step - 1)],
+            send_sem=spread_sem.at[0],
+            recv_sem=spread_sem.at[1],
+            device_id=member_device(step),
+            device_id_type=MESH,
+        ).start()
+    for index in range(early, len(offsets)):
+        send_rows(index)
+    for index in range(2, len(sources)):
+        build_tiles(index)
+
     wait_all(spread_ref, spread_sem.at[1], members - 1)
-    reduced = local_ref[piece_rows(member)]
+    reduced = mine_ref[piece_rows(member)]
     for step in range(members - 1):
         reduced += spread_ref[pl.ds(step * piece, piece)].astype(jnp.float32)
 
@@ -219,7 +242,7 @@
                 dst_ref=across_ref.at[step],
                 send_sem=across_sem.at[0, step],
                 recv_sem=across_sem.at[1, step],
-                device_id=device(across_peer(step)),
+                device_id=across_device(step),
                 device_id_type=MESH,
             )
             copy.start()
@@ -228,20 +251,18 @@
             across_copies[step - 1].wait()
             reduced += across_ref[step]
 
-    gathered_ref[piece_rows(member)] = reduced.astype(jnp.bfloat16)
-
-    def send_reduced(step, carry):
+    base = replica * share + member * piece
+    own_piece = pl.ds(pl.multiple_of(base, piece), piece)
+    gathered_ref[own_piece] = reduced.astype(jnp.bfloat16)
+    for step in range(1, members):
         pltpu.make_async_remote_copy(
-            src_ref=gathered_ref.at[piece_rows(member)],
-            dst_ref=gathered_ref.at[piece_rows(member)],
+            src_ref=gathered_ref.at[own_piece],
+            dst_ref=gathered_ref.at[own_piece],
             send_sem=gather_sem.at[0],
             recv_sem=gather_sem.at[1],
-            device_id=device(group_peer(step)),
+            device_id=member_device(step),
             device_id_type=MESH,
         ).start()
-        return carry
-
-    lax.fori_loop(1, members, send_reduced, 0)
 
     for copy in row_copies:
         copy.wait_recv()
@@ -259,13 +280,27 @@
             )
             copy.start()
             partial_copies.append(copy)
+    wait_all(gathered_ref, gather_sem.at[1], members - 1)
+    share_copies = []
+    for step in range(1, replicas):
+        copy = pltpu.make_async_remote_copy(
+            src_ref=gathered_ref.at[share_rows(replica)],
+            dst_ref=gathered_ref.at[share_rows(replica)],
+            send_sem=share_send_sem.at[step - 1],
+            recv_sem=share_recv_sem.at[step - 1],
+            device_id=replica_device(step),
+            device_id_type=MESH,
+        )
+        copy.start()
+        share_copies.append(copy)
     owned = product(0, 1, 0, len(sources))
     for step, copy in enumerate(partial_copies):
         copy.wait_recv()
         owned += landed_ref[pl.ds(step * tile_side, tile_side)]
     features_ref[...] = (owned * inverse).astype(jnp.bfloat16)
 
-    wait_all(gathered_ref, gather_sem.at[1], members - 1)
+    for copy in share_copies:
+        copy.wait_recv()
     raw = gathered_ref[...].astype(jnp.float32)
     total = jnp.sum(jnp.sum(raw * raw, axis=0, keepdims=True), axis=1, keepdims=True)
     scale = jnp.minimum(1.0, 128.0 / jnp.sqrt(total + 1e-06))
@@ -276,7 +311,7 @@
 
     wait_all(spread_ref, spread_sem.at[0], members - 1)
     wait_all(gathered_ref, gather_sem.at[0], members - 1)
-    for copy in row_copies + partial_copies:
+    for copy in shared_copies + row_copies + partial_copies + share_copies:
         copy.wait_send()
 
 
@@ -286,9 +321,10 @@
     tile_side, hidden = grad_out.shape
     slots, depth = neighbors.shape[3], neighbors.shape[4]
     packed = hidden * hidden // LANES
-    members = min(blocks * replicas, packed // PACKED_ROWS)
-    groups = blocks * replicas // members
-    piece = packed // members
+    share = packed // replicas
+    members = min(blocks, share // PACKED_ROWS)
+    groups = blocks // members
+    piece = share // members
     offsets = []
     for distance in range(1, REACH + 1):
         for offset in (distance, -distance):
@@ -314,8 +350,10 @@
             pltpu.VMEM((hidden, hidden), jnp.bfloat16),
             pltpu.VMEM((near, slots, depth, tile_side), jnp.int32),
             pltpu.VMEM((packed, LANES), jnp.float32),
-            pltpu.VMEM((packed, LANES), jnp.bfloat16),
-            pltpu.VMEM((packed, LANES), jnp.bfloat16),
+            pltpu.VMEM((others * share, LANES), jnp.float32),
+            pltpu.VMEM((share, LANES), jnp.float32),
+            pltpu.VMEM((share, LANES), jnp.bfloat16),
+            pltpu.VMEM((share, LANES), jnp.bfloat16),
             pltpu.VMEM((groups, piece, LANES), jnp.float32),
             pltpu.VMEM((packed, LANES), jnp.bfloat16),
             pltpu.VMEM((near * tile_side, hidden), jnp.bfloat16),
@@ -323,9 +361,13 @@
             pltpu.VMEM((others * tile_side, hidden), jnp.float32),
             pltpu.VMEM((others * tile_side, hidden), jnp.float32),
             pltpu.SemaphoreType.DMA((4 + near,)),
+            pltpu.SemaphoreType.DMA((others,)),
+            pltpu.SemaphoreType.DMA((others,)),
             pltpu.SemaphoreType.DMA((2,)),
             pltpu.SemaphoreType.DMA((2, groups)),
             pltpu.SemaphoreType.DMA((2,)),
+            pltpu.SemaphoreType.DMA((others,)),
+            pltpu.SemaphoreType.DMA((others,)),
             pltpu.SemaphoreType.DMA((near,)),
             pltpu.SemaphoreType.DMA((near,)),
             pltpu.SemaphoreType.DMA((others,)),

time: 24.3 us -> 24.7 us (1.016)
  Pallas kernels: 20.3 us -> 20.6 us
    pallas_call x1, Pallas kernels: 20.3 us -> 20.6 us  [on_device(): pl.pallas_call(functools.partial(kernel, blocks, replicas, members, tuple...]
where the time goes in v3:
time: 24.7 us; the launch traced here: 24.4 us
  Pallas kernels  20.6 us (83%)
  local copies, waits for them, and re-layouts  3.14 us (13%)
  between operations  0.64 us (3%)
    pallas_call x1, Pallas kernels, on_device(): pl.pallas_call(functools.partial(kernel, blocks, replicas, members, tuple...  20.6 us
    unnamed x2, local copies, waits for them, and re-layouts  3.14 us

profile of v3, /device:TPU:0, one launch (start us, length us, event | category | flops | bytes accessed | tf_op | source)
XLA Modules:
  0.0 24.4 jit_solution(5889988912797051605)
XLA Ops:
  0.6 20.6 %shard_map.95 = (bf16[128,256]{1,0:T(8,128)(2,1)}, f32[256,256]{1,0:T(8,128)}) custom-call(bf16[128,256]{1,0:T(8,128)(2,1)} %grad_out_hbm.1, bf16[128,256]{1,0:T(8,128)(2,1)} %preact_hbm.1, bf16[128,256]{1,0:T(8,128)(2,1)} %aggregated_hbm.1, bf16[256,256]{1,0:T(8,128)(2,1)} %weight_hbm.1, s32[1,128]{1,0:T(1,128)} %bitcast.3, ...), custom_call_target="tpu_custom_call" | custom-call | tf_op jit(solution)/shard_map/pallas_call | solution.py:338
  21.2 1.5 %copy.12 = bf16[128,256]{1,0:T(8,128)(2,1)} copy(bf16[128,256]{1,0:T(8,128)(2,1)} %get-tuple-element.4) | data formatting | bytes 131072
  22.7 1.7 %copy.13 = f32[256,256]{1,0:T(8,128)} copy(f32[256,256]{1,0:T(8,128)} %get-tuple-element.5) | data formatting | bytes 524288

commit v4 on v3

--- a/solution.py
+++ b/solution.py
@@ -42,6 +42,7 @@
     gathered_ref,
     rows_ref,
     tiles_ref,
+    begun_ref,
     partial_ref,
     landed_ref,
     load_sem,
@@ -120,10 +121,35 @@
 
     loads[0].wait()
     loads[1].wait()
-    loads[2].wait()
     grad_pre = jnp.where(
         preact_ref[...].astype(jnp.float32) > 0, grad_out_ref[...].astype(jnp.float32), 0.0
     ).astype(jnp.bfloat16)
+    loads[3].wait()
+    backward = lax.dot_general(
+        grad_pre, weight_ref[...], (((1,), (1,)), ((), ())), preferred_element_type=jnp.float32
+    )
+    rows_ref[pl.ds(0, tile_side)] = (backward * inverse).astype(jnp.bfloat16)
+
+    pl.semaphore_wait(barrier, len(greeted))
+
+    row_copies = []
+
+    def send_rows(index):
+        copy = pltpu.make_async_remote_copy(
+            src_ref=rows_ref.at[pl.ds(0, tile_side)],
+            dst_ref=rows_ref.at[pl.ds((index + 1) * tile_side, tile_side)],
+            send_sem=rows_send_sem.at[index],
+            recv_sem=rows_recv_sem.at[index],
+            device_id=near_device(offsets[index]),
+            device_id_type=MESH,
+        )
+        copy.start()
+        row_copies.append(copy)
+
+    for index in range(len(offsets)):
+        send_rows(index)
+
+    loads[2].wait()
     local = lax.dot_general(
         aggregated_ref[...], grad_pre, (((0,), (0,)), ((), ())), preferred_element_type=jnp.float32
     )
@@ -131,14 +157,6 @@
         rows = pl.ds(half * hidden, hidden)
         columns = local[:, half * LANES : (half + 1) * LANES]
         local_ref[rows] = columns
-    loads[3].wait()
-    backward = lax.dot_general(
-        grad_pre, weight_ref[...], (((1,), (1,)), ((), ())), preferred_element_type=jnp.float32
-    )
-    rows_ref[pl.ds(0, tile_side)] = (backward * inverse).astype(jnp.bfloat16)
-
-    pl.semaphore_wait(barrier, len(greeted))
-
     shared_copies = []
     for step in range(1, replicas):
         copy = pltpu.make_async_remote_copy(
@@ -151,24 +169,6 @@
         )
         copy.start()
         shared_copies.append(copy)
-
-    row_copies = []
-
-    def send_rows(index):
-        copy = pltpu.make_async_remote_copy(
-            src_ref=rows_ref.at[pl.ds(0, tile_side)],
-            dst_ref=rows_ref.at[pl.ds((index + 1) * tile_side, tile_side)],
-            send_sem=rows_send_sem.at[index],
-            recv_sem=rows_recv_sem.at[index],
-            device_id=near_device(offsets[index]),
-            device_id_type=MESH,
-        )
-        copy.start()
-        row_copies.append(copy)
-
-    early = len(offsets) // 2
-    for index in range(early):
-        send_rows(index)
 
     positions = lax.broadcasted_iota(jnp.int32, (tile_side, tile_side), 0)
 
@@ -223,8 +223,6 @@
             device_id=member_device(step),
             device_id_type=MESH,
         ).start()
-    for index in range(early, len(offsets)):
-        send_rows(index)
     for index in range(2, len(sources)):
         build_tiles(index)
 
@@ -264,11 +262,18 @@
             device_id_type=MESH,
         ).start()
 
-    for copy in row_copies:
+    early = len(sources) // 2 + 1
+    for copy in row_copies[: early - 1]:
+        copy.wait_recv()
+    begun_ref[...] = product(0, replicas, 0, early)
+    for copy in row_copies[early - 1 :]:
         copy.wait_recv()
     partial_copies = []
     if replicas > 1:
-        partial_ref[...] = product(1, replicas - 1, 0, len(sources))
+        others = pl.ds(tile_side, (replicas - 1) * tile_side)
+        partial_ref[...] = begun_ref[others] + product(
+            1, replicas - 1, early, len(sources) - early
+        )
         for step in range(1, replicas):
             copy = pltpu.make_async_remote_copy(
                 src_ref=partial_ref.at[pl.ds((step - 1) * tile_side, tile_side)],
@@ -293,7 +298,7 @@
         )
         copy.start()
         share_copies.append(copy)
-    owned = product(0, 1, 0, len(sources))
+    owned = begun_ref[pl.ds(0, tile_side)] + product(0, 1, early, len(sources) - early)
     for step, copy in enumerate(partial_copies):
         copy.wait_recv()
         owned += landed_ref[pl.ds(step * tile_side, tile_side)]
@@ -326,20 +331,21 @@
     groups = blocks // members
     piece = share // members
     offsets = []
-    for distance in range(1, REACH + 1):
+    for distance in range(REACH, 0, -1):
         for offset in (distance, -distance):
             if offset % blocks and offset % blocks not in [o % blocks for o in offsets]:
                 offsets.append(offset)
     near = len(offsets) + 1
     others = max(replicas - 1, 1)
+    held = functools.partial(pltpu.with_memory_space_constraint, memory_space=pltpu.HBM)
     hbm = pl.BlockSpec(memory_space=pltpu.HBM)
     vmem = pl.BlockSpec(memory_space=pltpu.VMEM)
     smem = pl.BlockSpec(memory_space=pltpu.SMEM)
     return pl.pallas_call(
         functools.partial(kernel, blocks, replicas, members, tuple(offsets)),
         out_shape=(
-            jax.ShapeDtypeStruct((tile_side, hidden), jnp.bfloat16),
-            jax.ShapeDtypeStruct((hidden, hidden), jnp.float32),
+            pltpu.VMEM((tile_side, hidden), jnp.bfloat16),
+            pltpu.VMEM((hidden, hidden), jnp.float32),
         ),
         in_specs=[hbm, hbm, hbm, hbm, vmem, hbm, smem, smem],
         out_specs=(vmem, vmem),
@@ -358,6 +364,7 @@
             pltpu.VMEM((packed, LANES), jnp.bfloat16),
             pltpu.VMEM((near * tile_side, hidden), jnp.bfloat16),
             pltpu.VMEM((replicas * tile_side, near * tile_side), jnp.bfloat16),
+            pltpu.VMEM((replicas * tile_side, hidden), jnp.float32),
             pltpu.VMEM((others * tile_side, hidden), jnp.float32),
             pltpu.VMEM((others * tile_side, hidden), jnp.float32),
             pltpu.SemaphoreType.DMA((4 + near,)),
@@ -374,17 +381,17 @@
             pltpu.SemaphoreType.DMA((others,)),
         ],
         compiler_params=pltpu.CompilerParams(
-            collective_id=0, has_side_effects=True, vmem_limit_bytes=63 * 1024 * 1024
+            collective_id=0, has_side_effects=True, vmem_limit_bytes=32 * 1024 * 1024
         ),
     )(
-        grad_out,
-        preact,
-        aggregated,
-        weight,
-        degree.reshape(1, tile_side),
-        neighbors,
-        jnp.swapaxes(tile_col, 2, 3),
-        tile_count,
+        held(grad_out),
+        held(preact),
+        held(aggregated),
+        held(weight),
+        held(degree.reshape(1, tile_side)),
+        held(neighbors),
+        held(jnp.swapaxes(tile_col, 2, 3)),
+        held(tile_count),
     )
 
 

time: 24.7 us -> 23 us (0.931)
  local copies, waits for them, and re-layouts: 3.14 us -> 1.33 us
    unnamed x2, local copies, waits for them, and re-layouts: 3.14 us -> 1.33 us
where the time goes in v4:
time: 23 us; the launch traced here: 22.8 us
  Pallas kernels  20.8 us (90%)
  local copies, waits for them, and re-layouts  1.33 us (6%)
  between operations  0.64 us (3%)
    pallas_call x1, Pallas kernels, on_device(): pl.pallas_call(functools.partial(kernel, blocks, replicas, members, tuple...  20.8 us
    unnamed x2, local copies, waits for them, and re-layouts  1.33 us

profile of v4, /device:TPU:0, one launch (start us, length us, event | category | flops | bytes accessed | tf_op | source)
XLA Modules:
  0.0 22.8 jit_solution(12358016262444756909)
XLA Ops:
  0.6 20.8 %shard_map.95 = (bf16[128,256]{1,0:T(8,128)(2,1)S(1)}, f32[256,256]{1,0:T(8,128)S(1)}) custom-call(bf16[128,256]{1,0:T(8,128)(2,1)} %grad_out_hbm.1, bf16[128,256]{1,0:T(8,128)(2,1)} %preact_hbm.1, bf16[128,256]{1,0:T(8,128)(2,1)} %aggregated_hbm.1, bf16[256,256]{1,0:T(8,128)(2,1)} %weight_hbm.1, s32[1,128]{1,0:T(1,128)} %bitcast.3, ...), custom_call_target="tpu_custom_call" | custom-call | tf_op jit(solution)/shard_map/pallas_call | solution.py:344
  21.4 0.6 %copy.12 = bf16[128,256]{1,0:T(8,128)(2,1)} copy(bf16[128,256]{1,0:T(8,128)(2,1)S(1)} %get-tuple-element.2) | data formatting | bytes 131072
  22.1 0.7 %copy.13 = f32[256,256]{1,0:T(8,128)} copy(f32[256,256]{1,0:T(8,128)S(1)} %get-tuple-element.3) | data formatting | bytes 524288

commit v5 on v1

--- a/solution.py
+++ b/solution.py
@@ -40,6 +40,7 @@
     gathered_ref,
     rows_ref,
     tiles_ref,
+    begun_ref,
     partial_ref,
     landed_ref,
     load_sem,
@@ -79,6 +80,27 @@
     def piece_rows(index):
         return pl.ds(pl.multiple_of(index * piece, piece), piece)
 
+    loads = [
+        pltpu.make_async_copy(source, target, load_sem.at[index])
+        for index, (source, target) in enumerate(
+            (
+                (grad_out_hbm, grad_out_ref),
+                (preact_hbm, preact_ref),
+                (aggregated_hbm, aggregated_ref),
+                (weight_hbm, weight_ref),
+            )
+        )
+    ]
+    sources = [block] + [lax.rem(block - offset + blocks, blocks) for offset in offsets]
+    for index, source in enumerate(sources):
+        loads.append(
+            pltpu.make_async_copy(
+                neighbors_hbm.at[0, 0, source], listed_ref.at[index], load_sem.at[4 + index]
+            )
+        )
+    for load in loads:
+        load.start()
+
     barrier = pltpu.get_barrier_semaphore()
 
     def greet(target):
@@ -98,27 +120,6 @@
         for step in range(1, replicas):
             greet(replica_device(step))
         greeted += groups - 1 + len(offsets) + replicas - 1
-
-    loads = [
-        pltpu.make_async_copy(source, target, load_sem.at[index])
-        for index, (source, target) in enumerate(
-            (
-                (grad_out_hbm, grad_out_ref),
-                (preact_hbm, preact_ref),
-                (aggregated_hbm, aggregated_ref),
-                (weight_hbm, weight_ref),
-            )
-        )
-    ]
-    sources = [block] + [lax.rem(block - offset + blocks, blocks) for offset in offsets]
-    for index, source in enumerate(sources):
-        loads.append(
-            pltpu.make_async_copy(
-                neighbors_hbm.at[0, 0, source], listed_ref.at[index], load_sem.at[4 + index]
-            )
-        )
-    for load in loads:
-        load.start()
 
     inverse = 1.0 / jnp.sqrt(degree_ref[...].astype(jnp.float32))
     inverse = jnp.transpose(jnp.broadcast_to(inverse, (tile_side, tile_side)))[:, :1]
@@ -172,24 +173,43 @@
         copy.start()
         row_copies.append(copy)
 
-    positions = lax.broadcasted_iota(jnp.int32, (tile_side, tile_side), 0)
-    for index, source in enumerate(sources):
-        loads[4 + index].wait()
-        totals = [jnp.zeros((tile_side, tile_side), jnp.float32) for _ in range(replicas)]
+    chunk = tile_side // 2
+    positions = lax.broadcasted_iota(jnp.int32, (chunk, tile_side), 0)
+    for load in loads[4:]:
+        load.wait()
+
+    def build_tiles(index, carry):
+        source = sources[0]
+        for other in range(1, len(sources)):
+            source = jnp.where(index == other, sources[other], source)
+        lanes = pl.ds(pl.multiple_of(index * tile_side, tile_side), tile_side)
+        weights = []
         for slot in range(slots):
-            counted = jnp.zeros((tile_side, tile_side), jnp.float32)
-            for entry in range(depth):
-                listed = listed_ref[index, slot, pl.ds(entry, 1), :]
-                counted += jnp.where(listed == positions, 1.0, 0.0)
             column = column_ref[0, 0, slot, source]
             present = slot < count_ref[0, 0, source]
+            weights.append([
+                jnp.where(
+                    jnp.logical_and(present, column == lax.rem(replica + step, replicas)), 1.0, 0.0
+                )
+                for step in range(replicas)
+            ])
+        for start in range(0, tile_side, chunk):
+            totals = [None] * replicas
+            for slot in range(slots):
+                counted = jnp.zeros((chunk, tile_side), jnp.float32)
+                for entry in range(depth):
+                    listed = listed_ref[index, slot, pl.ds(entry, 1), :] - start
+                    counted += jnp.where(listed == positions, 1.0, 0.0)
+                for step in range(replicas):
+                    term = counted * weights[slot][step]
+                    totals[step] = term if slot == 0 else totals[step] + term
             for step in range(replicas):
-                here = jnp.logical_and(present, column == lax.rem(replica + step, replicas))
-                totals[step] += counted * jnp.where(here, 1.0, 0.0)
-        for step in range(replicas):
-            tiles_ref[
-                pl.ds(step * tile_side, tile_side), pl.ds(index * tile_side, tile_side)
-            ] = totals[step].astype(jnp.bfloat16)
+                tiles_ref[pl.ds(step * tile_side + start, chunk), lanes] = totals[step].astype(
+                    jnp.bfloat16
+                )
+        return carry
+
+    lax.fori_loop(0, len(sources), build_tiles, 0)
 
     def product(first_row, row_count, first_source, source_count):
         return jnp.dot(
@@ -243,11 +263,18 @@
 
     lax.fori_loop(1, members, send_reduced, 0)
 
-    for copy in row_copies:
+    early = len(sources) // 2 + 1
+    for copy in row_copies[: early - 1]:
+        copy.wait_recv()
+    begun_ref[...] = product(0, replicas, 0, early)
+    for copy in row_copies[early - 1 :]:
         copy.wait_recv()
     partial_copies = []
     if replicas > 1:
-        partial_ref[...] = product(1, replicas - 1, 0, len(sources))
+        others = pl.ds(tile_side, (replicas - 1) * tile_side)
+        partial_ref[...] = begun_ref[others] + product(
+            1, replicas - 1, early, len(sources) - early
+        )
         for step in range(1, replicas):
             copy = pltpu.make_async_remote_copy(
                 src_ref=partial_ref.at[pl.ds((step - 1) * tile_side, tile_side)],
@@ -259,7 +286,7 @@
             )
             copy.start()
             partial_copies.append(copy)
-    owned = product(0, 1, 0, len(sources))
+    owned = begun_ref[pl.ds(0, tile_side)] + product(0, 1, early, len(sources) - early)
     for step, copy in enumerate(partial_copies):
         copy.wait_recv()
         owned += landed_ref[pl.ds(step * tile_side, tile_side)]
@@ -290,20 +317,21 @@
     groups = blocks * replicas // members
     piece = packed // members
     offsets = []
-    for distance in range(1, REACH + 1):
+    for distance in range(REACH, 0, -1):
         for offset in (distance, -distance):
             if offset % blocks and offset % blocks not in [o % blocks for o in offsets]:
                 offsets.append(offset)
     near = len(offsets) + 1
     others = max(replicas - 1, 1)
+    held = functools.partial(pltpu.with_memory_space_constraint, memory_space=pltpu.HBM)
     hbm = pl.BlockSpec(memory_space=pltpu.HBM)
     vmem = pl.BlockSpec(memory_space=pltpu.VMEM)
     smem = pl.BlockSpec(memory_space=pltpu.SMEM)
     return pl.pallas_call(
         functools.partial(kernel, blocks, replicas, members, tuple(offsets)),
         out_shape=(
-            jax.ShapeDtypeStruct((tile_side, hidden), jnp.bfloat16),
-            jax.ShapeDtypeStruct((hidden, hidden), jnp.float32),
+            pltpu.VMEM((tile_side, hidden), jnp.bfloat16),
+            pltpu.VMEM((hidden, hidden), jnp.float32),
         ),
         in_specs=[hbm, hbm, hbm, hbm, vmem, hbm, smem, smem],
         out_specs=(vmem, vmem),
@@ -320,6 +348,7 @@
             pltpu.VMEM((packed, LANES), jnp.bfloat16),
             pltpu.VMEM((near * tile_side, hidden), jnp.bfloat16),
             pltpu.VMEM((replicas * tile_side, near * tile_side), jnp.bfloat16),
+            pltpu.VMEM((replicas * tile_side, hidden), jnp.float32),
             pltpu.VMEM((others * tile_side, hidden), jnp.float32),
             pltpu.VMEM((others * tile_side, hidden), jnp.float32),
             pltpu.SemaphoreType.DMA((4 + near,)),
@@ -335,14 +364,14 @@
             collective_id=0, has_side_effects=True, vmem_limit_bytes=32 * 1024 * 1024
         ),
     )(
-        grad_out,
-        preact,
-        aggregated,
-        weight,
-        degree.reshape(1, tile_side),
-        neighbors,
-        jnp.swapaxes(tile_col, 2, 3),
-        tile_count,
+        held(grad_out),
+        held(preact),
+        held(aggregated),
+        held(weight),
+        held(degree.reshape(1, tile_side)),
+        held(neighbors),
+        held(jnp.swapaxes(tile_col, 2, 3)),
+        held(tile_count),
     )
 
 

time: 26.6 us -> 21.2 us (0.80)
  local copies, waits for them, and re-layouts: 6.33 us -> 1.33 us
    unnamed x18 -> x2, local copies, waits for them, and re-layouts: 6.33 us -> 1.33 us
where the time goes in v5:
time: 21.2 us; the launch traced here: 21.1 us
  Pallas kernels  19.1 us (90%)
  local copies, waits for them, and re-layouts  1.33 us (6%)
  between operations  0.64 us (3%)
    pallas_call x1, Pallas kernels, on_device(): pl.pallas_call(functools.partial(kernel, blocks, replicas, members, tuple...  19.1 us
    unnamed x2, local copies, waits for them, and re-layouts  1.33 us

profile of v5, /device:TPU:0, one launch (start us, length us, event | category | flops | bytes accessed | tf_op | source)
XLA Modules:
  0.0 21.1 jit_solution(8194026103474093302)
XLA Ops:
  0.6 19.1 %shard_map.95 = (bf16[128,256]{1,0:T(8,128)(2,1)S(1)}, f32[256,256]{1,0:T(8,128)S(1)}) custom-call(bf16[128,256]{1,0:T(8,128)(2,1)} %grad_out_hbm.1, bf16[128,256]{1,0:T(8,128)(2,1)} %preact_hbm.1, bf16[128,256]{1,0:T(8,128)(2,1)} %aggregated_hbm.1, bf16[256,256]{1,0:T(8,128)(2,1)} %weight_hbm.1, s32[1,128]{1,0:T(1,128)} %bitcast.3, ...), custom_call_target="tpu_custom_call" | custom-call | tf_op jit(solution)/shard_map/pallas_call | solution.py:330
  19.7 0.6 %copy.12 = bf16[128,256]{1,0:T(8,128)(2,1)} copy(bf16[128,256]{1,0:T(8,128)(2,1)S(1)} %get-tuple-element.2) | data formatting | bytes 131072
  20.4 0.7 %copy.13 = f32[256,256]{1,0:T(8,128)} copy(f32[256,256]{1,0:T(8,128)S(1)} %get-tuple-element.3) | data formatting | bytes 524288

commit v6 on v5

--- a/solution.py
+++ b/solution.py
@@ -53,23 +53,34 @@
     partial_recv_sem,
 ):
     block, replica = lax.axis_index("blk"), lax.axis_index("rep")
-    me = block * replicas + replica
-    groups = blocks * replicas // members
-    group, member = me // members, lax.rem(me, members)
+    side = members // replicas
+    groups = blocks // side
+    group, place = block // side, lax.rem(block, side)
+    member = place * replicas + replica
     tile_side, hidden = grad_out_ref.shape
     slots = listed_ref.shape[1]
     depth = listed_ref.shape[2]
     piece = part_ref.shape[0] // members
     halves = hidden // LANES
 
-    def device(flat):
-        return (flat // replicas, lax.rem(flat, replicas))
-
-    def group_peer(step):
-        return group * members + lax.rem(member + step, members)
-
-    def across_peer(step):
-        return lax.rem(group + step, groups) * members + member
+    def across_device(step):
+        return (lax.rem(group + step, groups) * side + place, replica)
+
+    def each_member(act):
+        def at_distance(step, carry):
+            peer_place = lax.rem(place + step, side)
+            for other in range(replicas):
+                act(
+                    (group * side + peer_place, other),
+                    peer_place * replicas + other,
+                    (step - 1) * replicas + replica,
+                )
+            return carry
+
+        lax.fori_loop(1, side, at_distance, 0)
+        for step in range(1, replicas):
+            other = lax.rem(replica + step, replicas)
+            act((block, other), place * replicas + other, (side - 1) * replicas + step - 1)
 
     def near_device(offset):
         return (lax.rem(block + offset + blocks, blocks), replica)
@@ -106,15 +117,11 @@
     def greet(target):
         pl.semaphore_signal(barrier, inc=1, device_id=target, device_id_type=MESH)
 
-    def greet_member(step, carry):
-        greet(device(group_peer(step)))
-        return carry
-
-    lax.fori_loop(1, members, greet_member, 0)
+    each_member(lambda target, index, slot: greet(target))
     greeted = members - 1
     if groups > 1:
         for step in range(1, groups):
-            greet(device(across_peer(step)))
+            greet(across_device(step))
         for offset in offsets:
             greet(near_device(offset))
         for step in range(1, replicas):
@@ -138,27 +145,25 @@
         columns = local[:, half * LANES : (half + 1) * LANES]
         local_ref[rows] = columns
         part_ref[rows] = columns.astype(jnp.bfloat16)
+    pl.semaphore_wait(barrier, greeted)
+
+    def send_piece(target, index, slot):
+        pltpu.make_async_remote_copy(
+            src_ref=part_ref.at[piece_rows(index)],
+            dst_ref=spread_ref.at[piece_rows(slot)],
+            send_sem=spread_sem.at[0],
+            recv_sem=spread_sem.at[1],
+            device_id=target,
+            device_id_type=MESH,
+        ).start()
+
+    each_member(send_piece)
+
     loads[3].wait()
     backward = lax.dot_general(
         grad_pre, weight_ref[...], (((1,), (1,)), ((), ())), preferred_element_type=jnp.float32
     )
     rows_ref[pl.ds(0, tile_side)] = (backward * inverse).astype(jnp.bfloat16)
-
-    pl.semaphore_wait(barrier, greeted)
-
-    def send_piece(step, carry):
-        peer = group_peer(step)
-        pltpu.make_async_remote_copy(
-            src_ref=part_ref.at[piece_rows(lax.rem(peer, members))],
-            dst_ref=spread_ref.at[piece_rows(step - 1)],
-            send_sem=spread_sem.at[0],
-            recv_sem=spread_sem.at[1],
-            device_id=device(peer),
-            device_id_type=MESH,
-        ).start()
-        return carry
-
-    lax.fori_loop(1, members, send_piece, 0)
 
     row_copies = []
     for index, offset in enumerate(offsets):
@@ -209,7 +214,7 @@
                 )
         return carry
 
-    lax.fori_loop(0, len(sources), build_tiles, 0)
+    lax.fori_loop(0, 2, build_tiles, 0)
 
     def product(first_row, row_count, first_source, source_count):
         return jnp.dot(
@@ -239,7 +244,7 @@
                 dst_ref=across_ref.at[step],
                 send_sem=across_sem.at[0, step],
                 recv_sem=across_sem.at[1, step],
-                device_id=device(across_peer(step)),
+                device_id=across_device(step),
                 device_id_type=MESH,
             )
             copy.start()
@@ -250,18 +255,18 @@
 
     gathered_ref[piece_rows(member)] = reduced.astype(jnp.bfloat16)
 
-    def send_reduced(step, carry):
+    def send_reduced(target, index, slot):
         pltpu.make_async_remote_copy(
             src_ref=gathered_ref.at[piece_rows(member)],
             dst_ref=gathered_ref.at[piece_rows(member)],
             send_sem=gather_sem.at[0],
             recv_sem=gather_sem.at[1],
-            device_id=device(group_peer(step)),
+            device_id=target,
             device_id_type=MESH,
         ).start()
-        return carry
-
-    lax.fori_loop(1, members, send_reduced, 0)
+
+    each_member(send_reduced)
+    lax.fori_loop(2, len(sources), build_tiles, 0)
 
     early = len(sources) // 2 + 1
     for copy in row_copies[: early - 1]:

time: 21.2 us -> 21.2 us (level)
  no operation moved by 1% of the time
where the time goes in v6:
time: 21.2 us; the launch traced here: 21 us
  Pallas kernels  19.1 us (90%)
  local copies, waits for them, and re-layouts  1.33 us (6%)
  between operations  0.64 us (3%)
    pallas_call x1, Pallas kernels, on_device(): pl.pallas_call(functools.partial(kernel, blocks, replicas, members, tuple...  19.1 us
    unnamed x2, local copies, waits for them, and re-layouts  1.33 us

profile of v6, /device:TPU:0, one launch (start us, length us, event | category | flops | bytes accessed | tf_op | source)
XLA Modules:
  0.0 21.0 jit_solution(8770256771766150859)
XLA Ops:
  0.6 19.1 %shard_map.95 = (bf16[128,256]{1,0:T(8,128)(2,1)S(1)}, f32[256,256]{1,0:T(8,128)S(1)}) custom-call(bf16[128,256]{1,0:T(8,128)(2,1)} %grad_out_hbm.1, bf16[128,256]{1,0:T(8,128)(2,1)} %preact_hbm.1, bf16[128,256]{1,0:T(8,128)(2,1)} %aggregated_hbm.1, bf16[256,256]{1,0:T(8,128)(2,1)} %weight_hbm.1, s32[1,128]{1,0:T(1,128)} %bitcast.3, ...), custom_call_target="tpu_custom_call" | custom-call | tf_op jit(solution)/shard_map/pallas_call | solution.py:335
  19.7 0.6 %copy.12 = bf16[128,256]{1,0:T(8,128)(2,1)} copy(bf16[128,256]{1,0:T(8,128)(2,1)S(1)} %get-tuple-element.2) | data formatting | bytes 131072
  20.3 0.7 %copy.13 = f32[256,256]{1,0:T(8,128)} copy(f32[256,256]{1,0:T(8,128)S(1)} %get-tuple-element.3) | data formatting | bytes 524288

commit v7 on v6

--- a/solution.py
+++ b/solution.py
@@ -27,7 +27,7 @@
     column_ref,
     count_ref,
     features_ref,
-    weight_out_ref,
+    raw_ref,
     grad_out_ref,
     preact_ref,
     aggregated_ref,
@@ -298,18 +298,29 @@
     features_ref[...] = (owned * inverse).astype(jnp.bfloat16)
 
     wait_all(gathered_ref, gather_sem.at[1], members - 1)
-    raw = gathered_ref[...].astype(jnp.float32)
-    total = jnp.sum(jnp.sum(raw * raw, axis=0, keepdims=True), axis=1, keepdims=True)
-    scale = jnp.minimum(1.0, 128.0 / jnp.sqrt(total + 1e-06))
-    for half in range(halves):
-        weight_out_ref[:, pl.ds(half * LANES, LANES)] = (
-            raw[half * hidden : (half + 1) * hidden] * scale
-        )
+    raw_ref[...] = gathered_ref[...]
 
     wait_all(spread_ref, spread_sem.at[0], members - 1)
     wait_all(gathered_ref, gather_sem.at[0], members - 1)
     for copy in row_copies + partial_copies:
         copy.wait_send()
+
+
+def finish(features_ref, raw_ref, features_hbm, weight_hbm, weight_ref, sem):
+    features_copy = pltpu.make_async_copy(features_ref, features_hbm, sem.at[0])
+    features_copy.start()
+    hidden = weight_ref.shape[0]
+    raw = raw_ref[...].astype(jnp.float32)
+    total = jnp.sum(jnp.sum(raw * raw, axis=0, keepdims=True), axis=1, keepdims=True)
+    scale = jnp.minimum(1.0, 128.0 / jnp.sqrt(total + 1e-06))
+    for half in range(hidden // LANES):
+        weight_ref[:, pl.ds(half * LANES, LANES)] = (
+            raw[half * hidden : (half + 1) * hidden] * scale
+        )
+    weight_copy = pltpu.make_async_copy(weight_ref, weight_hbm, sem.at[1])
+    weight_copy.start()
+    features_copy.wait()
+    weight_copy.wait()
 
 
 def on_device(
@@ -332,11 +343,11 @@
     hbm = pl.BlockSpec(memory_space=pltpu.HBM)
     vmem = pl.BlockSpec(memory_space=pltpu.VMEM)
     smem = pl.BlockSpec(memory_space=pltpu.SMEM)
-    return pl.pallas_call(
+    features, raw = pl.pallas_call(
         functools.partial(kernel, blocks, replicas, members, tuple(offsets)),
         out_shape=(
             pltpu.VMEM((tile_side, hidden), jnp.bfloat16),
-            pltpu.VMEM((hidden, hidden), jnp.float32),
+            pltpu.VMEM((packed, LANES), jnp.bfloat16),
         ),
         in_specs=[hbm, hbm, hbm, hbm, vmem, hbm, smem, smem],
         out_specs=(vmem, vmem),
@@ -378,6 +389,19 @@
         held(jnp.swapaxes(tile_col, 2, 3)),
         held(tile_count),
     )
+    return pl.pallas_call(
+        finish,
+        out_shape=(
+            jax.ShapeDtypeStruct((tile_side, hidden), jnp.bfloat16),
+            jax.ShapeDtypeStruct((hidden, hidden), jnp.float32),
+        ),
+        in_specs=[vmem, vmem],
+        out_specs=(hbm, hbm),
+        scratch_shapes=[
+            pltpu.VMEM((hidden, hidden), jnp.float32),
+            pltpu.SemaphoreType.DMA((2,)),
+        ],
+    )(features, raw)
 
 
 def solution(mesh):

time: 21.2 us -> 22.8 us (1.075)
  Pallas kernels: 19.1 us -> 20.7 us
    pallas_call x0 -> x1, Pallas kernels: none -> 1.85 us  [on_device(): pl.pallas_call(finish, out_shape=(jax.ShapeDtypeStruct((tile_side, hidden...]
    unnamed x2 -> x4, local copies, waits for them, and re-layouts: 1.33 us -> 1.26 us
where the time goes in v7:
time: 22.8 us; the launch traced here: 22.6 us
  Pallas kernels  20.7 us (91%)
  local copies, waits for them, and re-layouts  1.26 us (6%)
  between operations  0.65 us (3%)
    pallas_call x1, Pallas kernels, on_device(): pl.pallas_call(functools.partial(kernel, blocks, replicas, members, tuple...  18.9 us
    pallas_call x1, Pallas kernels, on_device(): pl.pallas_call(finish, out_shape=(jax.ShapeDtypeStruct((tile_side, hidden...  1.85 us
    unnamed x4, local copies, waits for them, and re-layouts  1.26 us

profile of v7, /device:TPU:0, one launch (start us, length us, event | category | flops | bytes accessed | tf_op | source)
XLA Modules:
  0.0 22.6 jit_solution(16831857038466256524)
XLA Ops:
  0.6 18.9 %shard_map.95 = (bf16[128,256]{1,0:T(8,128)(2,1)S(1)}, bf16[512,128]{1,0:T(8,128)(2,1)S(1)}) custom-call(bf16[128,256]{1,0:T(8,128)(2,1)} %grad_out_hbm.1, bf16[128,256]{1,0:T(8,128)(2,1)} %preact_hbm.1, bf16[128,256]{1,0:T(8,128)(2,1)} %aggregated_hbm.1, bf16[256,256]{1,0:T(8,128)(2,1)} %weight_hbm.1, s32[1,128]{1,0:T(1,128)} %bitcast.3, ...), custom_call_target="tpu_custom_call" | custom-call | tf_op jit(solution)/shard_map/pallas_call | solution.py:346
  19.5 0.0 copy-start
  19.5 0.6 %copy-done = bf16[512,128]{1,0:T(8,128)(2,1)} copy-done((bf16[512,128]{1,0:T(8,128)(2,1)}, bf16[512,128]{1,0:T(8,128)(2,1)S(1)}, u32[]{:S(2)}) %copy-start) | copy-done | bytes 131096
  20.2 0.0 copy-start.1
  20.2 0.6 %copy-done.1 = bf16[128,256]{1,0:T(8,128)(2,1)} copy-done((bf16[128,256]{1,0:T(8,128)(2,1)}, bf16[128,256]{1,0:T(8,128)(2,1)S(1)}, u32[]{:S(2)}) %copy-start.1) | copy-done | bytes 65560
  20.8 1.8 %shard_map.96 = (bf16[128,256]{1,0:T(8,128)(2,1)}, f32[256,256]{1,0:T(8,128)}) custom-call(bf16[128,256]{1,0:T(8,128)(2,1)} %copy-done.1, bf16[512,128]{1,0:T(8,128)(2,1)} %copy-done), custom_call_target="tpu_custom_call" | custom-call | tf_op jit(solution)/shard_map/pallas_call | solution.py:392
Async XLA Ops:
  19.5 0.6 %copy-start = (bf16[512,128]{1,0:T(8,128)(2,1)}, bf16[512,128]{1,0:T(8,128)(2,1)S(1)}, u32[]{:S(2)}) copy-start(bf16[512,128]{1,0:T(8,128)(2,1)S(1)} %get-tuple-element.5.raw_ref) | copy-start | bytes 393220
  20.2 0.6 %copy-start.1 = (bf16[128,256]{1,0:T(8,128)(2,1)}, bf16[128,256]{1,0:T(8,128)(2,1)S(1)}, u32[]{:S(2)}) copy-start(bf16[128,256]{1,0:T(8,128)(2,1)S(1)} %get-tuple-element.4.features_ref) | copy-start | bytes 196612
